TPU v7x, 32 devices: a whole 2x2x4 slice. The times are simulated.
32 devices in a mesh: dp: 16 (over z, y, x), stream: 2 (over core).
Axes of the slice: x: 2, y: 2, z: 4, core: 2. Of those that a mesh axis runs over, the one named last changes fastest.
Arguments:
- tokens: bfloat16 [16384, 512], P(('dp', 'stream')), may hold values from -6 to 6
- memory: bfloat16 [16384, 512], P(('dp', 'stream')), may hold values from -6 to 6
- cotangent: bfloat16 [16384, 512], P(('dp', 'stream')), may hold values from -6 to 6
- segments: int32 [16384], P(('dp', 'stream')), may hold values from 0 to 1039, as said below
- padding: int32 [16384], P(('dp', 'stream')), may hold values from 0 to 1, as said below
- priority: int32 [16384], P(('dp', 'stream')), may hold values from 0 to 4095
- threshold: int32 [16384], P(('dp', 'stream')), may hold values from 0 to 4096
- master: float32 [8192, 512], P(('dp', 'stream'))
- momentum: float32 [8192, 512], P(('dp', 'stream')), may hold values from -80 to 80
- vectors: float32 [8704], replicated
- vec_first: float32 [8704], replicated, may hold values from -224 to 224
- vec_second: float32 [8704], replicated, may hold values from 1.47456 to 5.89824
- step_count: int32 [1], replicated, may hold values from 2 to 20
Outputs:
- layer_out: bfloat16 [16384, 512], P(('dp', 'stream'))
- input_grad: float32 [16384, 512], P(('dp', 'stream'))
- memory_grad: float32 [16384, 512], P(('dp', 'stream'))
- new_momentum: float32 [8192, 512], P(('dp', 'stream'))
- new_master: float32 [8192, 512], P(('dp', 'stream'))
- new_vectors: float32 [8704], replicated
- new_vec_first: float32 [8704], replicated
- new_vec_second: float32 [8704], replicated
Inputs may be any that keep to these rules, and one draw needn't show every extreme that they name: `segments`: ids never fall and never cross an aligned block of 1024 rows. A block holds one whole document of 1024 tokens (some blocks in every draw) or sentences of 16 to 44 tokens, whose last one may be cut off by the block's end. `padding`: 1 exactly on the rows of a sentence cut off by its block's end.
All inputs are finite; a program needn't handle non-finite values.
Results may differ from a plain program's by a relative error of at most 0.025.
The roundings to bfloat16 on the way count: a program that leaves them out, or rounds other values in their place, can miss the bound.
Values may be sent and summed in bfloat16 or wider, within the bound.
A program may use at most 256 MiB of HBM per device.

v0:
```python
import jax
import jax.numpy as jnp
from jax import lax
from jax.sharding import PartitionSpec as P

D = 512
HEADS = 8
HEAD = 64
FF = 2048
NS_A = 3.4445
NS_B = -4.775
NS_C = 2.0315
MUON_RATE = 0.8
ADAM_RATE = 0.2
ADAM_DECAY = 0.01
HIGH = lax.Precision.HIGHEST


def partner(block, axis, stride):
    count = lax.axis_size(axis)
    route = []
    for low in range(count):
        high = low | 1 << stride
        if high != low and high < count:
            route += [(low, high), (high, low)]
    return lax.ppermute(block, axis, route)


def plain_dot(left_mat, right_mat):
    return jnp.dot(left_mat, right_mat, preferred_element_type=jnp.float32)


def lead_dot(left_mat, right_mat):
    return lax.dot_general(
        left_mat, right_mat, (((0,), (0,)), ((), ())), preferred_element_type=jnp.float32
    )


def last_dot(left_mat, right_mat):
    return lax.dot_general(
        left_mat, right_mat, (((1,), (1,)), ((), ())), preferred_element_type=jnp.float32
    )


def high_dot(left_mat, right_mat):
    return jnp.dot(left_mat, right_mat, precision=lax.Precision.HIGH)


def exact_lead(left_mat, right_mat):
    return lax.dot_general(left_mat, right_mat, (((0,), (0,)), ((), ())), precision=HIGH)


def split_rows(all_rows):
    attn_w = all_rows[: 8 * D].reshape(8, D, D)
    return (attn_w, all_rows[8 * D : 8 * D + FF], all_rows[8 * D + FF :])


def norm_forward(values, gain_vec, shift_vec):
    center = values - jnp.mean(values, axis=-1, keepdims=True)
    spread = lax.rsqrt(jnp.mean(center * center, axis=-1, keepdims=True) + 1e-05)
    normed = center * spread
    return (normed * gain_vec + shift_vec, normed, spread)


def norm_backward(normed, spread, gain_vec, grad_out):
    grad_gain = jnp.sum(grad_out * normed, axis=0)
    grad_shift = jnp.sum(grad_out, axis=0)
    scaled = grad_out * gain_vec
    grad_in = spread * (
        scaled
        - jnp.mean(scaled, axis=-1, keepdims=True)
        - normed * jnp.mean(scaled * normed, axis=-1, keepdims=True)
    )
    return (grad_in, grad_gain, grad_shift)


def split_heads(matrix):
    return matrix.reshape(matrix.shape[0], HEADS, HEAD)


def block_scores(queries, keys_all, visible):
    scores = jnp.einsum(
        "qhe,khe->hqk",
        split_heads(queries),
        split_heads(keys_all),
        preferred_element_type=jnp.float32,
    )
    return jnp.where(visible[None], scores * HEAD ** (-0.5), -1e30)


def attend_forward(queries, keys_all, values_all, visible):
    scores = block_scores(queries, keys_all, visible)
    row_max = jnp.max(scores, axis=-1, keepdims=True)
    expo = jnp.exp(scores - row_max)
    row_total = jnp.sum(expo, axis=-1, keepdims=True)
    weights_low = (expo / row_total).astype(jnp.bfloat16)
    mixed = jnp.einsum(
        "hqk,khe->qhe", weights_low, split_heads(values_all), preferred_element_type=jnp.float32
    )
    return (mixed.reshape(queries.shape[0], HEADS * HEAD), row_max + jnp.log(row_total))


def attend_backward(queries, keys_all, values_all, visible, logsum, grad_out):
    probs = jnp.exp(block_scores(queries, keys_all, visible) - logsum)
    grad_heads = split_heads(grad_out)
    grad_probs = jnp.einsum(
        "qhe,khe->hqk", grad_heads, split_heads(values_all), preferred_element_type=jnp.float32
    )
    inner_sum = jnp.sum(grad_probs * probs, axis=-1, keepdims=True)
    grad_scores = (probs * (grad_probs - inner_sum) * HEAD ** (-0.5)).astype(jnp.bfloat16)
    grad_q = jnp.einsum(
        "hqk,khe->qhe", grad_scores, split_heads(keys_all), preferred_element_type=jnp.float32
    )
    grad_k = jnp.einsum(
        "hqk,qhe->khe", grad_scores, split_heads(queries), preferred_element_type=jnp.float32
    )
    grad_v = jnp.einsum(
        "hqk,qhe->khe", probs.astype(jnp.bfloat16), grad_heads, preferred_element_type=jnp.float32
    )
    key_count = keys_all.shape[0]
    return (
        grad_q.reshape(queries.shape[0], HEADS * HEAD),
        grad_k.reshape(key_count, HEADS * HEAD),
        grad_v.reshape(key_count, HEADS * HEAD),
    )


def attend_all(queries, keys_all, values_all, visible):
    mixed, logsum = attend_forward(queries, keys_all, values_all, visible)
    logsums = [logsum]
    return (mixed, logsums)


def attend_back_all(queries, keys_all, values_all, visible, logsums, grad_out):
    block_rows = min(512, queries.shape[0])
    grad_q_parts = []
    grad_keys = jnp.zeros(keys_all.shape, jnp.float32)
    grad_values = jnp.zeros(values_all.shape, jnp.float32)
    for block_index, begin_row in enumerate(range(0, queries.shape[0], block_rows)):
        grad_q, grad_k, grad_v = attend_backward(
            queries, keys_all, values_all, visible, logsums[block_index], grad_out
        )
        grad_q_parts.append(grad_q)
        grad_keys = grad_k
        grad_values = grad_v
    return (grad_q_parts[0], grad_keys, grad_values)


def per_device(
    tokens,
    memory,
    cotangent,
    segments,
    padding,
    priority,
    threshold,
    master,
    momentum,
    vectors,
    vec_first,
    vec_second,
    step_count,
):

    def vector_part(position):
        return vectors[position * D : (position + 1) * D]

    low_master = master.astype(jnp.bfloat16)
    attn_w, w_in, w_out = split_rows(
        lax.all_gather(low_master, ("dp", "stream"), axis=0, tiled=True)
    )
    tokens_f32 = tokens.astype(jnp.float32)
    ln_one, normed_one, spread_one = norm_forward(tokens_f32, vector_part(0), vector_part(1))
    h_one = ln_one.astype(jnp.bfloat16)
    queries = (plain_dot(h_one, attn_w[0]) + vector_part(6)).astype(jnp.bfloat16)
    keys_own = plain_dot(h_one, attn_w[1]).astype(jnp.bfloat16)
    values_own = (plain_dot(h_one, attn_w[2]) + vector_part(7)).astype(jnp.bfloat16)
    mem_keys = plain_dot(memory, attn_w[5]).astype(jnp.bfloat16)
    mem_values = (plain_dot(memory, attn_w[6]) + vector_part(10)).astype(jnp.bfloat16)
    keys_all, values_all, mem_keys_all, mem_values_all = (
        lax.all_gather(keys_own, "stream", axis=0, tiled=True),
        lax.all_gather(values_own, "stream", axis=0, tiled=True),
        lax.all_gather(mem_keys, "stream", axis=0, tiled=True),
        lax.all_gather(mem_values, "stream", axis=0, tiled=True),
    )
    seg_all, pad_all, prio_all = (
        lax.all_gather(segments, "stream", axis=0, tiled=True),
        lax.all_gather(padding, "stream", axis=0, tiled=True),
        lax.all_gather(priority, "stream", axis=0, tiled=True),
    )
    own_rows = queries.shape[0]
    place = jnp.arange(own_rows, dtype=jnp.int32) + lax.axis_index("stream") * own_rows
    key_place = jnp.arange(seg_all.shape[0], dtype=jnp.int32)
    diagonal = place[:, None] == key_place[None, :]
    same_seg = segments[:, None] == seg_all[None, :]
    open_key = (pad_all == 0)[None, :]
    vis_self = same_seg & ((prio_all[None, :] < threshold[:, None]) & open_key | diagonal)
    vis_cross = same_seg & (open_key | diagonal)
    attn_out, lse_one = attend_all(queries, keys_all, values_all, vis_self)
    attn_low = attn_out.astype(jnp.bfloat16)
    res_one = tokens_f32 + plain_dot(attn_low, attn_w[3]) + vector_part(8)
    ln_two, normed_two, spread_two = norm_forward(res_one, vector_part(2), vector_part(3))
    h_two = ln_two.astype(jnp.bfloat16)
    cross_q = (plain_dot(h_two, attn_w[4]) + vector_part(9)).astype(jnp.bfloat16)
    cross_out, lse_two = attend_all(cross_q, mem_keys_all, mem_values_all, vis_cross)
    cross_low = cross_out.astype(jnp.bfloat16)
    res_two = res_one + plain_dot(cross_low, attn_w[7]) + vector_part(11)
    ln_three, normed_three, spread_three = norm_forward(res_two, vector_part(4), vector_part(5))
    h_three = ln_three.astype(jnp.bfloat16)
    pre_act = last_dot(h_three, w_in) + vectors[13 * D :]
    hidden = jnp.maximum(pre_act, 0.0).astype(jnp.bfloat16)
    layer_out = (res_two + plain_dot(hidden, w_out) + vector_part(12)).astype(jnp.bfloat16)
    grad_out_w = lead_dot(hidden, cotangent)
    grad_bias_out = jnp.sum(cotangent.astype(jnp.float32), axis=0)
    grad_hidden = last_dot(cotangent, w_out)
    grad_pre = jnp.where(pre_act > 0, grad_hidden, 0.0).astype(jnp.bfloat16)
    grad_bias_hidden = jnp.sum(grad_pre.astype(jnp.float32), axis=0)
    grad_in_w = lead_dot(grad_pre, h_three)
    grad_ln_three, grad_gain_three, grad_shift_three = norm_backward(
        normed_three, spread_three, vector_part(4), plain_dot(grad_pre, w_in)
    )
    grad_res_two = cotangent.astype(jnp.float32) + grad_ln_three
    grad_res_two_low = grad_res_two.astype(jnp.bfloat16)
    grad_bias_cross_o = jnp.sum(grad_res_two, axis=0)
    grad_cross_o_w = lead_dot(cross_low, grad_res_two_low)
    grad_cross = last_dot(grad_res_two_low, attn_w[7]).astype(jnp.bfloat16)
    grad_cq, grad_mk_all, grad_mv_all = attend_back_all(
        cross_q, mem_keys_all, mem_values_all, vis_cross, lse_two, grad_cross
    )
    grad_cq_low = grad_cq.astype(jnp.bfloat16)
    grad_bias_cq = jnp.sum(grad_cq_low.astype(jnp.float32), axis=0)
    grad_cq_w = lead_dot(h_two, grad_cq_low)
    grad_ln_two, grad_gain_two, grad_shift_two = norm_backward(
        normed_two, spread_two, vector_part(2), last_dot(grad_cq_low, attn_w[4])
    )
    grad_res_one = grad_res_two + grad_ln_two
    grad_res_one_low = grad_res_one.astype(jnp.bfloat16)
    grad_bias_o = jnp.sum(grad_res_one, axis=0)
    grad_o_w = lead_dot(attn_low, grad_res_one_low)
    grad_attn = last_dot(grad_res_one_low, attn_w[3]).astype(jnp.bfloat16)
    grad_q, grad_k_all, grad_v_all = attend_back_all(
        queries, keys_all, values_all, vis_self, lse_one, grad_attn
    )
    grad_k, grad_v, grad_mk, grad_mv = (
        lax.psum_scatter(grad_k_all, "stream", scatter_dimension=0, tiled=True),
        lax.psum_scatter(grad_v_all, "stream", scatter_dimension=0, tiled=True),
        lax.psum_scatter(grad_mk_all, "stream", scatter_dimension=0, tiled=True),
        lax.psum_scatter(grad_mv_all, "stream", scatter_dimension=0, tiled=True),
    )
    grad_q_low = grad_q.astype(jnp.bfloat16)
    grad_k_low = grad_k.astype(jnp.bfloat16)
    grad_v_low = grad_v.astype(jnp.bfloat16)
    grad_mk_low = grad_mk.astype(jnp.bfloat16)
    grad_mv_low = grad_mv.astype(jnp.bfloat16)
    grad_h_one = (
        last_dot(grad_q_low, attn_w[0])
        + last_dot(grad_k_low, attn_w[1])
        + last_dot(grad_v_low, attn_w[2])
    )
    grad_ln_one, grad_gain_one, grad_shift_one = norm_backward(
        normed_one, spread_one, vector_part(0), grad_h_one
    )
    input_grad = grad_res_one + grad_ln_one
    memory_grad = last_dot(grad_mk_low, attn_w[5]) + last_dot(grad_mv_low, attn_w[6])
    stacked = jnp.concatenate(
        [
            lead_dot(h_one, grad_q_low),
            lead_dot(h_one, grad_k_low),
            lead_dot(h_one, grad_v_low),
            grad_o_w,
            grad_cq_w,
            lead_dot(memory, grad_mk_low),
            lead_dot(memory, grad_mv_low),
            grad_cross_o_w,
            grad_in_w,
            grad_out_w,
        ],
        axis=0,
    )
    vec_local = jnp.concatenate(
        [
            grad_gain_one,
            grad_shift_one,
            grad_gain_two,
            grad_shift_two,
            grad_gain_three,
            grad_shift_three,
            jnp.sum(grad_q_low.astype(jnp.float32), axis=0),
            jnp.sum(grad_v_low.astype(jnp.float32), axis=0),
            grad_bias_o,
            grad_bias_cq,
            jnp.sum(grad_mv_low.astype(jnp.float32), axis=0),
            grad_bias_cross_o,
            grad_bias_out,
            grad_bias_hidden,
        ],
        axis=0,
    )
    grad_rows = lax.psum_scatter(stacked, ("dp", "stream"), scatter_dimension=0, tiled=True)
    grad_vec = lax.psum(vec_local, ("dp", "stream"))
    opt_rows = master.shape[0]
    device_index = lax.axis_index(("dp", "stream"))
    start_row = device_index * opt_rows
    in_ffn = start_row >= 8 * D
    att_bits = (D // opt_rows).bit_length() - 1
    ffn_bits = (FF // opt_rows).bit_length() - 1
    own_bits = jnp.where(in_ffn, ffn_bits, att_bits)
    new_momentum = 0.5 * momentum + grad_rows

    def gram_total(partial_value):
        for bit_pos in range(ffn_bits):
            other = partner(partial_value, ("dp", "stream"), bit_pos)
            partial_value = partial_value + jnp.where(bit_pos < own_bits, other, 0.0)
        return partial_value

    gram_first = gram_total(exact_lead(new_momentum, new_momentum))
    divisor = jnp.sqrt(jnp.trace(gram_first)) + 1e-07
    gram = gram_first / (divisor * divisor)
    unit = jnp.eye(D, dtype=jnp.float32)
    chain = None
    for turn in range(5):
        poly = NS_A * unit + NS_B * gram + NS_C * high_dot(gram, gram)
        chain = poly if chain is None else high_dot(chain, poly)
        if turn < 4:
            gram = high_dot(high_dot(gram, poly), poly)
    current = high_dot(new_momentum / divisor, chain)
    rate = MUON_RATE * jnp.where(in_ffn, (FF / D) ** 0.5, 1.0)
    new_master = master - rate * current
    count = step_count[0].astype(jnp.float32)
    new_first = 0.5 * vec_first + 0.5 * grad_vec
    new_second = 0.999 * vec_second + 0.001 * grad_vec * grad_vec
    first_fix = new_first / (1.0 - jnp.power(0.5, count))
    second_fix = new_second / (1.0 - jnp.power(0.999, count))
    new_vectors = vectors - ADAM_RATE * (
        first_fix / (jnp.sqrt(second_fix) + 1e-08) + ADAM_DECAY * vectors
    )
    return (
        layer_out,
        input_grad,
        memory_grad,
        new_momentum,
        new_master,
        new_vectors,
        new_first,
        new_second,
    )


def solution(mesh):
    return jax.shard_map(
        per_device,
        mesh=mesh,
        in_specs=(
            P(("dp", "stream"), None),
            P(("dp", "stream"), None),
            P(("dp", "stream"), None),
            P(("dp", "stream")),
            P(("dp", "stream")),
            P(("dp", "stream")),
            P(("dp", "stream")),
            P(("dp", "stream"), None),
            P(("dp", "stream"), None),
            P(),
            P(),
            P(),
            P(),
        ),
        out_specs=(
            P(("dp", "stream"), None),
            P(("dp", "stream"), None),
            P(("dp", "stream"), None),
            P(("dp", "stream"), None),
            P(("dp", "stream"), None),
            P(),
            P(),
            P(),
        ),
        check_vma=False,
    )
```

profile of v0, /device:TPU:0, one launch (start us, length us, event | category | flops | bytes accessed | tf_op | source)
XLA Modules:
  0.0 707.6 jit_solution(17345366208032327094)
XLA Ops:
  12.1 79.5 %all-gather.9.cloned.1.call-done = bf16[8192,512]{1,0:T(8,128)(2,1)} async-done(((bf16[256,512]{1,0:T(8,128)(2,1)}), bf16[8192,512]{1,0:T(8,128)(2,1)}) %all-gather.9.cloned.1.call-update) | async-done | bytes 8388624 | tf_op jit(solution)/shard_map/all_gather | solution.py:170
  116.7 3.2 fusion.153
  119.9 6.1 copy-done.1
  126.0 3.7 fusion.8
  131.2 8.2 %fusion.81 = bf16[8,64,512]{2,1,0:T(8,128)(2,1)S(1)} fusion(bf16[1024,8,64]{0,2,1:T(8,128)(2,1)S(1)} %bitcast.115, f32[8,512,1024]{2,1,0:T(8,128)} %copy-done.1, f32[8,512]{1,0:T(8,128)S(1)} %fusion.8, f32[8,512]{1,0:T(8,128)S(1)} %get-tuple-element.67), kind=kOutput, calls=%fused_computation.108 | convolution fusion | flops 549715968 | bytes 18382848 | tf_op jit(solution)/shard_map/hqk,khe->qhe/dot_general | solution.py:97
  145.0 4.5 fusion.155
  149.5 5.7 copy-done.2
  155.2 3.7 fusion.9
  160.5 8.0 %fusion.80 = bf16[8,64,512]{2,1,0:T(8,128)(2,1)S(1)} fusion(bf16[1024,8,64]{0,2,1:T(8,128)(2,1)S(1)} %bitcast.117, f32[8,512,1024]{2,1,0:T(8,128)} %copy-done.2, f32[8,512]{1,0:T(8,128)S(1)} %fusion.9, f32[8,512]{1,0:T(8,128)S(1)} %get-tuple-element.71), kind=kOutput, calls=%fused_computation.107 | convolution fusion | flops 549715968 | bytes 18382848 | tf_op jit(solution)/shard_map/hqk,khe->qhe/dot_general | solution.py:97
  179.8 3.8 fusion.158
  193.0 9.3 %fusion.163 = f32[8,512,1024]{2,1,0:T(8,128)} fusion(bf16[512,8,64]{0,2,1:T(8,128)(2,1)S(1)} %bitcast.119, bf16[1024,8,64]{0,2,1:T(8,128)(2,1)} %bitcast.118), kind=kOutput, calls=%fused_computation.238 | convolution fusion | flops 536870912 | bytes 18350080 | tf_op jit(solution)/shard_map/qhe,khe->hqk/dot_general | solution.py:106
  202.3 30.8 %convert_reduce_fusion.4 = (f32[8,64]{1,0:T(8,128)S(1)}, bf16[8,64,512]{2,1,0:T(8,128)(2,1)}) fusion(bf16[1024,8,64]{0,2,1:T(8,128)(2,1)} %bitcast.126, f32[8,512,1024]{2,1,0:T(8,128)} %fusion.163, f32[8,512,1024]{2,1,0:T(8,128)} %copy-done.2, f32[8,512]{1,0:T(8,128)S(1)} %log_add_fusion.1), kind=kOutput, calls=%fused_computation.127 | convolution fusion | flops 567022080 | bytes 35145728 | tf_op jit(solution)/shard_map/hqk,khe->qhe/dot_general | solution.py:111
  245.2 9.3 %fusion.164 = f32[8,512,1024]{2,1,0:T(8,128)} fusion(bf16[512,8,64]{0,2,1:T(8,128)(2,1)S(1)} %bitcast.121, bf16[1024,8,64]{0,2,1:T(8,128)(2,1)} %bitcast.116), kind=kOutput, calls=%fused_computation.239 | convolution fusion | flops 536870912 | bytes 18350080 | tf_op jit(solution)/shard_map/qhe,khe->hqk/dot_general | solution.py:106
  254.5 30.9 %fusion.19 = f32[8,64,1024]{2,1,0:T(8,128)} fusion(bf16[512,8,64]{0,2,1:T(8,128)(2,1)} %bitcast.136, f32[8,512,1024]{2,1,0:T(8,128)} %fusion.164, f32[8,512,1024]{2,1,0:T(8,128)} %copy-done.1, f32[8,512]{1,0:T(8,128)S(1)} %log_add_fusion), kind=kOutput, calls=%fused_computation.22 | convolution fusion | flops 566236160 | bytes 36192256 | tf_op jit(solution)/shard_map/hqk,qhe->khe/dot_general | solution.py:114
  285.5 10.7 %fusion.24 = f32[8,64,1024]{2,1,0:T(8,128)} fusion(bf16[512,8,64]{0,2,1:T(8,128)(2,1)} %bitcast.122, f32[8,512,1024]{2,1,0:T(8,128)} %copy-done.1, f32[8,512]{1,0:T(8,128)S(1)} %log_add_fusion), kind=kOutput, calls=%fused_computation.24 | convolution fusion | flops 545259520 | bytes 19415040 | tf_op jit(solution)/shard_map/hqk,qhe->khe/dot_general | solution.py:117
  296.3 30.9 %fusion.13 = f32[8,64,1024]{2,1,0:T(8,128)} fusion(bf16[512,8,64]{0,2,1:T(8,128)(2,1)} %bitcast.138, f32[8,512,1024]{2,1,0:T(8,128)} %fusion.163, f32[8,512,1024]{2,1,0:T(8,128)} %copy-done.2, f32[8,512]{1,0:T(8,128)S(1)} %log_add_fusion.1), kind=kOutput, calls=%fused_computation.20 | convolution fusion | flops 566236160 | bytes 36192256 | tf_op jit(solution)/shard_map/hqk,qhe->khe/dot_general | solution.py:114
  327.3 10.7 %fusion.26 = f32[8,64,1024]{2,1,0:T(8,128)} fusion(bf16[512,8,64]{0,2,1:T(8,128)(2,1)} %bitcast.120, f32[8,512,1024]{2,1,0:T(8,128)} %copy-done.2, f32[8,512]{1,0:T(8,128)S(1)} %log_add_fusion.1), kind=kOutput, calls=%fused_computation.25 | convolution fusion | flops 545259520 | bytes 19415040 | tf_op jit(solution)/shard_map/hqk,qhe->khe/dot_general | solution.py:117
  338.1 30.6 %convert_reduce_fusion.6 = (f32[8,64]{1,0:T(8,128)S(1)}, bf16[8,64,512]{2,1,0:T(8,128)(2,1)}) fusion(bf16[1024,8,64]{0,2,1:T(8,128)(2,1)} %bitcast.124, f32[8,512,1024]{2,1,0:T(8,128)} %fusion.164, f32[8,512,1024]{2,1,0:T(8,128)} %copy-done.1, f32[8,512]{1,0:T(8,128)S(1)} %log_add_fusion), kind=kOutput, calls=%fused_computation.129 | convolution fusion | flops 567022080 | bytes 35145728 | tf_op jit(solution)/shard_map/hqk,khe->qhe/dot_general | solution.py:111
  390.4 5.0 convolution_dynamic-update-slice_fusion.1
  395.4 5.5 convolution_dynamic-update-slice_fusion
  401.8 5.0 fusion.67
  415.6 166.6 %reduce-scatter.14.cloned.1.call-done = f32[256,512]{1,0:T(8,128)} async-done(((f32[8192,512]{1,0:T(8,128)}), f32[256,512]{1,0:T(8,128)}) %reduce-scatter.14.cloned.1.call-update) | async-done | bytes 524304 | tf_op jit(solution)/shard_map/reduce_scatter | solution.py:299
  595.7 59.5 %psum.7 = f32[8704]{0:T(1024)S(1)} all-reduce(f32[8704]{0:T(1024)S(1)} %constant_dynamic-update-slice_fusion.10), channel_id=1, replica_groups=mesh['dp'=16,'stream'=2] {'dp','stream'}, use_global_device_ids=true, to_apply=%region_38.39 | all-reduce | flops 8704 | bytes 69632 | tf_op jit(solution)/shard_map/psum | solution.py:300
  662.8 16.8 %collective-permute-done.2 = f32[512,512]{1,0:T(8,128)S(1)} collective-permute-done((f32[512,512]{1,0:T(8,128)S(1)}, f32[512,512]{1,0:T(8,128)S(1)}, u32[]{:S(2)}, u32[]{:S(2)}) %collective-permute-start.2) | collective-permute-done | bytes 1048608 | tf_op jit(solution)/shard_map/ppermute | solution.py:26
  (198 shorter events, 142.8 us)
Async XLA Ops:
  7.2 89.6 %copy-start = (bf16[512,512]{1,0:T(8,128)(2,1)S(1)}, bf16[512,512]{1,0:T(8,128)(2,1)}, u32[]{:S(2)}) copy-start(bf16[512,512]{1,0:T(8,128)(2,1)} %param.14) | copy-start | bytes 1572868
  7.2 84.5 %all-gather.9.cloned.1.call-start = ((), (), s32[]{:S(2)}) async-start(), calls=%async_computation.5 | async-start | bytes 8650752 | tf_op jit(solution)/shard_map/all_gather | solution.py:170
  9.1 105.5 %all-gather.13.cloned.1.call-start = ((), (), s32[]{:S(2)}) async-start(), calls=%async_computation.7 | async-start | bytes 1572864 | tf_op jit(solution)/shard_map/all_gather | solution.py:181
  94.2 35.6 %all-gather.11.cloned.1.call-start = ((), (), s32[]{:S(2)}) async-start(), calls=%async_computation.6 | async-start | bytes 1572864 | tf_op jit(solution)/shard_map/all_gather | solution.py:182
  96.7 44.7 %all-gather.17.cloned.1.call-start = ((), (), s32[]{:S(2)}) async-start(), calls=%async_computation.9 | async-start | bytes 1572864 | tf_op jit(solution)/shard_map/all_gather | solution.py:183
  99.1 59.9 %all-gather.15.cloned.1.call-start = ((), (), s32[]{:S(2)}) async-start(), calls=%async_computation.8 | async-start | bytes 1572864 | tf_op jit(solution)/shard_map/all_gather | solution.py:184
  112.9 258.3 %reduce-scatter.6.cloned.1.call-start = ((), (), s32[]{:S(2)}) async-start(), calls=%async_computation.10 | async-start | bytes 3145728 | tf_op jit(solution)/shard_map/reduce_scatter | solution.py:245
  114.6 15.1 %copy-start.22 = (bf16[512,512]{0,1:T(8,128)(2,1)}, bf16[512,512]{0,1:T(8,128)(2,1)S(1)}, u32[]{:S(2)}) copy-start(bf16[512,512]{0,1:T(8,128)(2,1)S(1)} %fusion.77) | copy-start | bytes 1572868
  142.9 15.9 %copy-start.15 = (bf16[1024,512]{0,1:T(8,128)(2,1)}, bf16[1024,512]{0,1:T(8,128)(2,1)S(1)}, u32[]{:S(2)}) copy-start(bf16[1024,512]{0,1:T(8,128)(2,1)S(1)} %copy.63) | copy-start | bytes 3145732
  145.0 13.9 %copy-start.23 = (bf16[512,512]{0,1:T(8,128)(2,1)}, bf16[512,512]{0,1:T(8,128)(2,1)S(1)}, u32[]{:S(2)}) copy-start(bf16[512,512]{0,1:T(8,128)(2,1)S(1)} %fusion.79) | copy-start | bytes 1572868
  160.5 15.1 %copy-start.17 = (bf16[512,512]{1,0:T(8,128)(2,1)S(1)}, bf16[512,512]{1,0:T(8,128)(2,1)}, u32[]{:S(2)}) copy-start(bf16[512,512]{1,0:T(8,128)(2,1)} %param.15) | copy-start | bytes 1572868
  168.5 15.2 %copy-start.20 = (bf16[8,64,512]{2,1,0:T(8,128)(2,1)}, bf16[8,64,512]{2,1,0:T(8,128)(2,1)S(1)}, u32[]{:S(2)}) copy-start(bf16[8,64,512]{2,1,0:T(8,128)(2,1)S(1)} %fusion.80) | copy-start | bytes 1572868
  285.5 88.5 %reduce-scatter.8.cloned.1.call-start = ((), (), s32[]{:S(2)}) async-start(), calls=%async_computation.11 | async-start | bytes 3145728 | tf_op jit(solution)/shard_map/reduce_scatter | solution.py:246
  296.3 85.8 %reduce-scatter.10.cloned.1.call-start = ((), (), s32[]{:S(2)}) async-start(), calls=%async_computation.12 | async-start | bytes 3145728 | tf_op jit(solution)/shard_map/reduce_scatter | solution.py:247
  327.2 57.6 %reduce-scatter.12.cloned.1.call-start = ((), (), s32[]{:S(2)}) async-start(), calls=%async_computation.13 | async-start | bytes 3145728 | tf_op jit(solution)/shard_map/reduce_scatter | solution.py:248
  338.0 244.1 %reduce-scatter.14.cloned.1.call-start = ((), (), s32[]{:S(2)}) async-start(), calls=%async_computation.14 | async-start | bytes 17301504 | tf_op jit(solution)/shard_map/reduce_scatter | solution.py:299
  400.9 185.6 %copy-start.4 = (f32[512,512]{0,1:T(8,128)S(1)}, f32[512,512]{0,1:T(8,128)}, u32[]{:S(2)}) copy-start(f32[512,512]{0,1:T(8,128)} %copy-done.3) | copy-start | bytes 3145732
  406.7 188.8 %copy-start.7 = (f32[512,512]{0,1:T(8,128)S(1)}, f32[512,512]{0,1:T(8,128)}, u32[]{:S(2)}) copy-start(f32[512,512]{0,1:T(8,128)} %reduce-scatter.12.cloned.1.call-done) | copy-start | bytes 3145732
  409.0 253.1 %copy-start.24 = (f32[8704]{0:T(1024)S(1)}, f32[8704]{0:T(1024)}, u32[]{:S(2)}) copy-start(f32[8704]{0:T(1024)} %param.22) | copy-start | bytes 104452
  409.0 253.1 %copy-start.25 = (f32[8704]{0:T(1024)S(1)}, f32[8704]{0:T(1024)}, u32[]{:S(2)}) copy-start(f32[8704]{0:T(1024)} %param.24) | copy-start | bytes 104452
  409.0 253.1 %copy-start.26 = (f32[8704]{0:T(1024)S(1)}, f32[8704]{0:T(1024)}, u32[]{:S(2)}) copy-start(f32[8704]{0:T(1024)} %param.23) | copy-start | bytes 104452
  586.2 6.8 collective-permute-start
  594.8 60.4 %collective-permute-start.1 = (f32[512,512]{1,0:T(8,128)S(1)}, f32[512,512]{1,0:T(8,128)}, u32[]{:S(2)}, u32[]{:S(2)}) collective-permute-start(f32[512,512]{1,0:T(8,128)S(1)} %select_add_fusion.7), channel_id=1, source_target_pairs={{0,2},{2,0},{1,3},{3,1},{4,6},{6,4},{5,7},{7,5},{8,10},{10,8},{9,1... | collective-permute-start | bytes 3145736 | tf_op jit(solution)/shard_map/ppermute | solution.py:26
  655.5 24.2 %collective-permute-start.2 = (f32[512,512]{1,0:T(8,128)S(1)}, f32[512,512]{1,0:T(8,128)S(1)}, u32[]{:S(2)}, u32[]{:S(2)}) collective-permute-start(f32[512,512]{1,0:T(8,128)S(1)} %select_add_fusion.6), channel_id=1, source_target_pairs={{0,4},{4,0},{1,5},{5,1},{2,6},{6,2},{3,7},{7,3},{8,12},{12,8},{9,1... | collective-permute-start | bytes 3145736 | tf_op jit(solution)/shard_map/ppermute | solution.py:26
  (17 other events, 93.7 us)
Sparse Core Ops, SparseCore 0:
  11.4 80.1 all-gather.8
  94.3 7.6 all-gather.12
  104.1 10.1 all-gather.10
  116.3 10.1 all-gather.16
  128.5 10.1 all-gather.14
  285.6 8.0 reduce-scatter.5
  296.4 10.3 reduce-scatter.7
  327.3 7.8 reduce-scatter.9
  338.1 10.2 reduce-scatter.11
  401.0 181.0 reduce-scatter.13
where the time goes:
time: 713 us; the launch traced here: 708 us
  matrix products  289 us (41%)
  waiting for transfers between devices  263 us (37%)
  blocking collectives  65.2 us (9%)
  local copies, waits for them, and re-layouts  40 us (6%)
  other arithmetic  30.2 us (4%)
  between operations  16.8 us (2%)
    reduce_scatter x1, waiting for transfers between devices, per_device(): lax.psum_scatter(stacked, ('dp', 'stream'), scatter_dimension=0, tiled=True)  167 us
    all_gather x1, waiting for transfers between devices, per_device(): lax.all_gather(low_master, ('dp', 'stream'), axis=0, tiled=True)  79.5 us
    dot_general x2, matrix products, attend_backward(): jnp.einsum('hqk,qhe->khe', grad_scores, split_heads(queries), preferred_e...  61.8 us
    dot_general x2, matrix products, attend_backward(): jnp.einsum('hqk,khe->qhe', grad_scores, split_heads(keys_all), preferred_...  61.4 us
    psum x1, blocking collectives, per_device(): grad_vec = lax.psum(vec_local, ('dp', 'stream'))  59.5 us
    dot_general x10, matrix products, lead_dot(): lax.dot_general(left_mat, right_mat, (((0,), (0,)), ((), ())), preferred_...  32.2 us
    unnamed x73, local copies, waits for them, and re-layouts  27.6 us
    dot_general x10, matrix products, plain_dot(): return jnp.dot(left_mat, right_mat, preferred_element_type=jnp.float32)  25.5 us
  transfers between devices with their start and end apart: 13, of which 3 were waited for; matrix products, arithmetic and copies ran while one was open for 25% of the time, Pallas kernels for 0%

commit v1 on v0

--- a/solution.py
+++ b/solution.py
@@ -297,7 +297,7 @@
         axis=0,
     )
     grad_rows = lax.psum_scatter(stacked, ("dp", "stream"), scatter_dimension=0, tiled=True)
-    grad_vec = lax.psum(vec_local, ("dp", "stream"))
+    grad_vec = jnp.sum(lax.all_gather(vec_local, ("dp", "stream")), axis=0)
     opt_rows = master.shape[0]
     device_index = lax.axis_index(("dp", "stream"))
     start_row = device_index * opt_rows

time: 713 us -> 687 us (0.964)
  blocking collectives: 65.2 us -> 5.72 us
  waiting for transfers between devices: 263 us -> 288 us
    psum x1 -> x0, blocking collectives: 59.5 us -> none  [per_device(): grad_vec = lax.psum(vec_local, ('dp', 'stream'))]
    all_gather x0 -> x1, waiting for transfers between devices: none -> 19.6 us  [per_device(): grad_vec = jnp.sum(lax.all_gather(vec_local, ('dp', 'stream')), axis=0)]
    unnamed x73 -> x72, local copies, waits for them, and re-layouts: 27.6 us -> 26.9 us
  transfers between devices with their start and end apart: 13 -> 14, of which waited for: 3 -> 5; matrix products, arithmetic and copies ran while one was open for 25% -> 26% of each run, Pallas kernels for 0% -> 0%
where the time goes in v1:
time: 687 us; the launch traced here: 681 us
  matrix products  292 us (43%)
  waiting for transfers between devices  288 us (42%)
  local copies, waits for them, and re-layouts  39.3 us (6%)
  other arithmetic  35.5 us (5%)
  between operations  16.4 us (2%)
    reduce_scatter x1, waiting for transfers between devices, per_device(): lax.psum_scatter(stacked, ('dp', 'stream'), scatter_dimension=0, tiled=True)  172 us
    all_gather x1, waiting for transfers between devices, per_device(): lax.all_gather(low_master, ('dp', 'stream'), axis=0, tiled=True)  79.5 us
    dot_general x2, matrix products, attend_backward(): jnp.einsum('hqk,qhe->khe', grad_scores, split_heads(queries), preferred_e...  61.8 us
    dot_general x2, matrix products, attend_backward(): jnp.einsum('hqk,khe->qhe', grad_scores, split_heads(keys_all), preferred_...  61.1 us
    dot_general x10, matrix products, lead_dot(): lax.dot_general(left_mat, right_mat, (((0,), (0,)), ((), ())), preferred_...  32.2 us
    unnamed x72, local copies, waits for them, and re-layouts  26.9 us
    dot_general x10, matrix products, plain_dot(): return jnp.dot(left_mat, right_mat, preferred_element_type=jnp.float32)  25.5 us
    dot_general x10, matrix products, last_dot(): lax.dot_general(left_mat, right_mat, (((1,), (1,)), ((), ())), preferred_...  22.8 us
  transfers between devices with their start and end apart: 14, of which 5 were waited for; matrix products, arithmetic and copies ran while one was open for 26% of the time, Pallas kernels for 0%

profile of v1, /device:TPU:0, one launch (start us, length us, event | category | flops | bytes accessed | tf_op | source)
XLA Modules:
  0.0 680.8 jit_solution(5933075405458351776)
XLA Ops:
  12.1 79.5 %all-gather.12.cloned.1.call-done = bf16[8192,512]{1,0:T(8,128)(2,1)} async-done(((bf16[256,512]{1,0:T(8,128)(2,1)}), bf16[8192,512]{1,0:T(8,128)(2,1)}) %all-gather.12.cloned.1.call-update) | async-done | bytes 8388624 | tf_op jit(solution)/shard_map/all_gather | solution.py:170
  116.6 3.2 fusion.153
  119.8 6.1 copy-done.1
  125.9 3.7 fusion.8
  131.2 8.2 %fusion.81 = bf16[8,64,512]{2,1,0:T(8,128)(2,1)S(1)} fusion(bf16[1024,8,64]{0,2,1:T(8,128)(2,1)S(1)} %bitcast.115, f32[8,512,1024]{2,1,0:T(8,128)} %copy-done.1, f32[8,512]{1,0:T(8,128)S(1)} %fusion.8, f32[8,512]{1,0:T(8,128)S(1)} %get-tuple-element.67), kind=kOutput, calls=%fused_computation.108 | convolution fusion | flops 549715968 | bytes 18382848 | tf_op jit(solution)/shard_map/hqk,khe->qhe/dot_general | solution.py:97
  144.9 4.5 fusion.155
  149.4 5.7 copy-done.2
  155.1 3.7 fusion.9
  160.4 8.0 %fusion.80 = bf16[8,64,512]{2,1,0:T(8,128)(2,1)S(1)} fusion(bf16[1024,8,64]{0,2,1:T(8,128)(2,1)S(1)} %bitcast.117, f32[8,512,1024]{2,1,0:T(8,128)} %copy-done.2, f32[8,512]{1,0:T(8,128)S(1)} %fusion.9, f32[8,512]{1,0:T(8,128)S(1)} %get-tuple-element.71), kind=kOutput, calls=%fused_computation.107 | convolution fusion | flops 549715968 | bytes 18382848 | tf_op jit(solution)/shard_map/hqk,khe->qhe/dot_general | solution.py:97
  179.8 3.8 fusion.158
  193.0 9.3 %fusion.163 = f32[8,512,1024]{2,1,0:T(8,128)} fusion(bf16[512,8,64]{0,2,1:T(8,128)(2,1)S(1)} %bitcast.119, bf16[1024,8,64]{0,2,1:T(8,128)(2,1)} %bitcast.118), kind=kOutput, calls=%fused_computation.238 | convolution fusion | flops 536870912 | bytes 18350080 | tf_op jit(solution)/shard_map/qhe,khe->hqk/dot_general | solution.py:106
  202.3 30.6 %convert_reduce_fusion.4 = (f32[8,64]{1,0:T(8,128)S(1)}, bf16[8,64,512]{2,1,0:T(8,128)(2,1)}) fusion(bf16[1024,8,64]{0,2,1:T(8,128)(2,1)} %bitcast.126, f32[8,512,1024]{2,1,0:T(8,128)} %fusion.163, f32[8,512,1024]{2,1,0:T(8,128)} %copy-done.2, f32[8,512]{1,0:T(8,128)S(1)} %log_add_fusion.1), kind=kOutput, calls=%fused_computation.127 | convolution fusion | flops 567022080 | bytes 35145728 | tf_op jit(solution)/shard_map/hqk,khe->qhe/dot_general | solution.py:111
  245.0 9.3 %fusion.164 = f32[8,512,1024]{2,1,0:T(8,128)} fusion(bf16[512,8,64]{0,2,1:T(8,128)(2,1)S(1)} %bitcast.121, bf16[1024,8,64]{0,2,1:T(8,128)(2,1)} %bitcast.116), kind=kOutput, calls=%fused_computation.239 | convolution fusion | flops 536870912 | bytes 18350080 | tf_op jit(solution)/shard_map/qhe,khe->hqk/dot_general | solution.py:106
  254.3 30.9 %fusion.19 = f32[8,64,1024]{2,1,0:T(8,128)} fusion(bf16[512,8,64]{0,2,1:T(8,128)(2,1)} %bitcast.136, f32[8,512,1024]{2,1,0:T(8,128)} %fusion.164, f32[8,512,1024]{2,1,0:T(8,128)} %copy-done.1, f32[8,512]{1,0:T(8,128)S(1)} %log_add_fusion), kind=kOutput, calls=%fused_computation.22 | convolution fusion | flops 566236160 | bytes 36192256 | tf_op jit(solution)/shard_map/hqk,qhe->khe/dot_general | solution.py:114
  285.2 10.7 %fusion.24 = f32[8,64,1024]{2,1,0:T(8,128)} fusion(bf16[512,8,64]{0,2,1:T(8,128)(2,1)} %bitcast.122, f32[8,512,1024]{2,1,0:T(8,128)} %copy-done.1, f32[8,512]{1,0:T(8,128)S(1)} %log_add_fusion), kind=kOutput, calls=%fused_computation.24 | convolution fusion | flops 545259520 | bytes 19415040 | tf_op jit(solution)/shard_map/hqk,qhe->khe/dot_general | solution.py:117
  296.0 30.9 %fusion.13 = f32[8,64,1024]{2,1,0:T(8,128)} fusion(bf16[512,8,64]{0,2,1:T(8,128)(2,1)} %bitcast.138, f32[8,512,1024]{2,1,0:T(8,128)} %fusion.163, f32[8,512,1024]{2,1,0:T(8,128)} %copy-done.2, f32[8,512]{1,0:T(8,128)S(1)} %log_add_fusion.1), kind=kOutput, calls=%fused_computation.20 | convolution fusion | flops 566236160 | bytes 36192256 | tf_op jit(solution)/shard_map/hqk,qhe->khe/dot_general | solution.py:114
  327.4 10.8 %fusion.26 = f32[8,64,1024]{2,1,0:T(8,128)} fusion(bf16[512,8,64]{0,2,1:T(8,128)(2,1)} %bitcast.120, f32[8,512,1024]{2,1,0:T(8,128)} %copy-done.2, f32[8,512]{1,0:T(8,128)S(1)} %log_add_fusion.1), kind=kOutput, calls=%fused_computation.25 | convolution fusion | flops 545259520 | bytes 19415040 | tf_op jit(solution)/shard_map/hqk,qhe->khe/dot_general | solution.py:117
  338.2 30.5 %convert_reduce_fusion.6 = (f32[8,64]{1,0:T(8,128)S(1)}, bf16[8,64,512]{2,1,0:T(8,128)(2,1)}) fusion(bf16[1024,8,64]{0,2,1:T(8,128)(2,1)} %bitcast.124, f32[8,512,1024]{2,1,0:T(8,128)} %fusion.164, f32[8,512,1024]{2,1,0:T(8,128)} %copy-done.1, f32[8,512]{1,0:T(8,128)S(1)} %log_add_fusion), kind=kOutput, calls=%fused_computation.129 | convolution fusion | flops 567022080 | bytes 35145728 | tf_op jit(solution)/shard_map/hqk,khe->qhe/dot_general | solution.py:111
  390.4 5.0 convolution_dynamic-update-slice_fusion.1
  395.4 5.4 convolution_dynamic-update-slice_fusion
  410.1 172.1 %reduce-scatter.14.cloned.1.call-done = f32[256,512]{1,0:T(8,128)} async-done(((f32[8192,512]{1,0:T(8,128)}), f32[256,512]{1,0:T(8,128)}) %reduce-scatter.14.cloned.1.call-update) | async-done | bytes 524304 | tf_op jit(solution)/shard_map/reduce_scatter | solution.py:299
  592.8 5.0 fusion.67
  602.7 16.0 %collective-permute-done.1 = f32[512,512]{1,0:T(8,128)} collective-permute-done((f32[512,512]{1,0:T(8,128)}, f32[512,512]{1,0:T(8,128)}, u32[]{:S(2)}, u32[]{:S(2)}) %collective-permute-start.1) | collective-permute-done | bytes 1048608 | tf_op jit(solution)/shard_map/ppermute | solution.py:26
  626.8 19.6 %all-gather.22.cloned.1.call-done = f32[32,1,8704]{2,1,0:T(1,128)} async-done(((f32[1,1,8704]{2,1,0:T(1,128)}), f32[32,1,8704]{2,1,0:T(1,128)}) %all-gather.22.cloned.1.call-update) | async-done | bytes 1114128 | tf_op jit(solution)/shard_map/all_gather | solution.py:300
  (200 shorter events, 151.9 us)
Async XLA Ops:
  7.2 89.6 %copy-start = (bf16[512,512]{1,0:T(8,128)(2,1)S(1)}, bf16[512,512]{1,0:T(8,128)(2,1)}, u32[]{:S(2)}) copy-start(bf16[512,512]{1,0:T(8,128)(2,1)} %param.14) | copy-start | bytes 1572868
  7.2 84.5 %all-gather.12.cloned.1.call-start = ((), (), s32[]{:S(2)}) async-start(), calls=%async_computation.5 | async-start | bytes 8650752 | tf_op jit(solution)/shard_map/all_gather | solution.py:170
  9.1 105.5 %all-gather.16.cloned.1.call-start = ((), (), s32[]{:S(2)}) async-start(), calls=%async_computation.7 | async-start | bytes 1572864 | tf_op jit(solution)/shard_map/all_gather | solution.py:181
  94.2 35.5 %all-gather.14.cloned.1.call-start = ((), (), s32[]{:S(2)}) async-start(), calls=%async_computation.6 | async-start | bytes 1572864 | tf_op jit(solution)/shard_map/all_gather | solution.py:182
  96.7 44.6 %all-gather.20.cloned.1.call-start = ((), (), s32[]{:S(2)}) async-start(), calls=%async_computation.9 | async-start | bytes 1572864 | tf_op jit(solution)/shard_map/all_gather | solution.py:183
  99.1 59.8 %all-gather.18.cloned.1.call-start = ((), (), s32[]{:S(2)}) async-start(), calls=%async_computation.8 | async-start | bytes 1572864 | tf_op jit(solution)/shard_map/all_gather | solution.py:184
  112.9 258.3 %reduce-scatter.6.cloned.1.call-start = ((), (), s32[]{:S(2)}) async-start(), calls=%async_computation.10 | async-start | bytes 3145728 | tf_op jit(solution)/shard_map/reduce_scatter | solution.py:245
  114.6 15.0 %copy-start.21 = (bf16[512,512]{0,1:T(8,128)(2,1)}, bf16[512,512]{0,1:T(8,128)(2,1)S(1)}, u32[]{:S(2)}) copy-start(bf16[512,512]{0,1:T(8,128)(2,1)S(1)} %fusion.77) | copy-start | bytes 1572868
  142.9 15.9 %copy-start.14 = (bf16[1024,512]{0,1:T(8,128)(2,1)}, bf16[1024,512]{0,1:T(8,128)(2,1)S(1)}, u32[]{:S(2)}) copy-start(bf16[1024,512]{0,1:T(8,128)(2,1)S(1)} %copy.63) | copy-start | bytes 3145732
  160.4 15.0 %copy-start.16 = (bf16[512,512]{1,0:T(8,128)(2,1)S(1)}, bf16[512,512]{1,0:T(8,128)(2,1)}, u32[]{:S(2)}) copy-start(bf16[512,512]{1,0:T(8,128)(2,1)} %param.15) | copy-start | bytes 1572868
  168.4 15.2 %copy-start.19 = (bf16[8,64,512]{2,1,0:T(8,128)(2,1)}, bf16[8,64,512]{2,1,0:T(8,128)(2,1)S(1)}, u32[]{:S(2)}) copy-start(bf16[8,64,512]{2,1,0:T(8,128)(2,1)S(1)} %fusion.80) | copy-start | bytes 1572868
  285.2 88.8 %reduce-scatter.8.cloned.1.call-start = ((), (), s32[]{:S(2)}) async-start(), calls=%async_computation.11 | async-start | bytes 3145728 | tf_op jit(solution)/shard_map/reduce_scatter | solution.py:246
  296.0 86.1 %reduce-scatter.10.cloned.1.call-start = ((), (), s32[]{:S(2)}) async-start(), calls=%async_computation.12 | async-start | bytes 3145728 | tf_op jit(solution)/shard_map/reduce_scatter | solution.py:247
  326.9 57.9 %reduce-scatter.12.cloned.1.call-start = ((), (), s32[]{:S(2)}) async-start(), calls=%async_computation.13 | async-start | bytes 3145728 | tf_op jit(solution)/shard_map/reduce_scatter | solution.py:248
  338.2 244.0 %reduce-scatter.14.cloned.1.call-start = ((), (), s32[]{:S(2)}) async-start(), calls=%async_computation.14 | async-start | bytes 17301504 | tf_op jit(solution)/shard_map/reduce_scatter | solution.py:299
  400.9 192.0 %copy-start.26 = (f32[512]{0:T(512)S(1)}, f32[512]{0:T(512)}, u32[]{:S(2)}) copy-start(f32[512]{0:T(512)} %get-tuple-element.52) | copy-start | bytes 6148
  400.9 198.9 %copy-start.4 = (f32[512,512]{0,1:T(8,128)S(1)}, f32[512,512]{0,1:T(8,128)}, u32[]{:S(2)}) copy-start(f32[512,512]{0,1:T(8,128)} %copy-done.3) | copy-start | bytes 3145732
  400.9 245.5 %all-gather.22.cloned.1.call-start = ((), (), s32[]{:S(2)}) async-start(), calls=%async_computation.15 | async-start | bytes 1148928 | tf_op jit(solution)/shard_map/all_gather | solution.py:300
  584.3 64.0 %copy-start.23 = (f32[8704]{0:T(1024)S(1)}, f32[8704]{0:T(1024)}, u32[]{:S(2)}) copy-start(f32[8704]{0:T(1024)} %param.22) | copy-start | bytes 104452
  584.3 64.1 %copy-start.24 = (f32[8704]{0:T(1024)S(1)}, f32[8704]{0:T(1024)}, u32[]{:S(2)}) copy-start(f32[8704]{0:T(1024)} %param.24) | copy-start | bytes 104452
  584.3 64.1 %copy-start.25 = (f32[8704]{0:T(1024)S(1)}, f32[8704]{0:T(1024)}, u32[]{:S(2)}) copy-start(f32[8704]{0:T(1024)} %param.23) | copy-start | bytes 104452
  586.3 3.0 collective-permute-start
  592.0 26.7 %collective-permute-start.1 = (f32[512,512]{1,0:T(8,128)}, f32[512,512]{1,0:T(8,128)}, u32[]{:S(2)}, u32[]{:S(2)}) collective-permute-start(f32[512,512]{1,0:T(8,128)} %select_add_fusion.7), channel_id=1, source_target_pairs={{0,2},{2,0},{1,3},{3,1},{4,6},{6,4},{5,7},{7,5},{8,10},{10,8},{9,1... | collective-permute-start | bytes 3145736 | tf_op jit(solution)/shard_map/ppermute | solution.py:26
  620.1 28.9 %collective-permute-start.2 = (f32[512,512]{1,0:T(8,128)S(1)}, f32[512,512]{1,0:T(8,128)S(1)}, u32[]{:S(2)}, u32[]{:S(2)}) collective-permute-start(f32[512,512]{1,0:T(8,128)S(1)} %select_add_fusion.6), channel_id=1, source_target_pairs={{0,4},{4,0},{1,5},{5,1},{2,6},{6,2},{3,7},{7,3},{8,12},{12,8},{9,1... | collective-permute-start | bytes 3145736 | tf_op jit(solution)/shard_map/ppermute | solution.py:26
  (17 other events, 100.7 us)
Sparse Core Ops, SparseCore 0:
  11.4 80.1 all-gather.11
  94.3 7.6 all-gather.15
  104.1 10.1 all-gather.13
  116.3 10.1 all-gather.19
  128.5 10.1 all-gather.17
  285.3 7.9 reduce-scatter.5
  296.1 10.4 reduce-scatter.7
  327.0 7.8 reduce-scatter.9
  338.3 9.7 reduce-scatter.11
  401.0 181.1 reduce-scatter.13
  588.7 57.6 all-gather.21
